TPU v7x, 32 devices: a whole 2x2x4 slice. The times are simulated.
32 devices in a mesh: section: 2 (over y), batch: 16 (over z, x, core).
Axes of the slice: x: 2, y: 2, z: 4, core: 2. Of those that a mesh axis runs over, the one named last changes fastest.
Arguments:
- images: bfloat16 [32, 64, 3072], P('batch', None, 'section'), may hold values from -1 to 1
- noise_draw: bfloat16 [32, 64, 3072], P('batch', None, 'section'), may hold values from -6 to 6
- cotangent: bfloat16 [32, 64, 3072], P('batch', None, 'section'), may hold values from -6 to 6
- hue_angle: float32 [32], P('batch'), may hold values from -0.5 to 0.5
- saturation: float32 [32], P('batch'), may hold values from 0.5 to 1.5
- timestep: int32 [32], P('batch'), may hold values from 50 to 199
- stem_weight: bfloat16 [3072, 1024], P('section'), may hold values from -0.109375 to 0.109375
- conv_weight: bfloat16 [2, 9216, 1024], P('section', 'batch'), may hold values from -0.0625 to 0.0625
- emb_weight: bfloat16 [2, 1024, 2048], P('section'), may hold values from -0.1875 to 0.1875
- head_weight: bfloat16 [1024, 3072], P(None, 'section'), may hold values from -0.1875 to 0.1875
Outputs:
- purified: bfloat16 [32, 64, 3072], P('batch', None, 'section')
- colour_grad: float32 [32, 2], P('batch')
All inputs are finite; a program needn't handle non-finite values.
Results may differ from a plain program's by a relative error of at most 0.039.
Values may be sent and summed in bfloat16 or wider, within the bound.
A program may use at most 128 MiB of HBM per device.

v0:
```python
import math
import jax
import jax.numpy as jnp
from jax import lax
from jax.sharding import PartitionSpec as P

CH = 1024
GROUPS = 32
TEMB = 1024
GRID = 8
TSTEPS = 1000
PV = 3072


def shifted(value, axis, steps):
    count = lax.axis_size(axis)
    pairs = [(source, (source + steps) % count) for source in range(count)]
    return lax.ppermute(value, axis, pairs)


def from_root(block, axis, holder):
    block = jnp.where(lax.axis_index(axis) == holder, block, jnp.zeros_like(block))
    return lax.psum(block, axis)


def noise_levels(timestep):
    beta_rates = jnp.linspace(0.0001, 0.02, TSTEPS, dtype=jnp.float32)
    levels = jnp.cumprod(1.0 - beta_rates)
    chosen = jnp.arange(TSTEPS, dtype=jnp.int32)[None, :] == timestep[:, None]
    return jnp.sum(jnp.where(chosen, levels[None, :], jnp.float32(0.0)), axis=1)


def time_features(timestep):
    half_width = TEMB // 2
    frequency = jnp.exp(-math.log(10000.0) * jnp.arange(half_width, dtype=jnp.float32) / half_width)
    angles = timestep.astype(jnp.float32)[:, None] * frequency[None, :]
    return jax.nn.silu(jnp.concatenate([jnp.cos(angles), jnp.sin(angles)], axis=1)).astype(
        jnp.bfloat16
    )


def colour_maps(hue_angle, saturation):
    grey_map = jnp.full((3, 3), 1.0 / 3.0, dtype=jnp.float32)
    rotate_map = jnp.eye(3, dtype=jnp.float32) - grey_map
    cross_map = jnp.array(
        [[0.0, -1.0, 1.0], [1.0, 0.0, -1.0], [-1.0, 1.0, 0.0]], dtype=jnp.float32
    ) / math.sqrt(3.0)
    cosine = jnp.cos(hue_angle)[:, None, None]
    sine_of = jnp.sin(hue_angle)[:, None, None]
    turning = cosine * rotate_map + sine_of * cross_map
    sat_scale = saturation[:, None, None]
    matrix = grey_map + sat_scale * turning
    hue_slope = sat_scale * (cosine * cross_map - sine_of * rotate_map)
    return (matrix, hue_slope, turning)


def apply_map(matrix, pixels):
    return jnp.sum(matrix[:, None, None, :, :] * pixels[:, :, :, None, :], axis=-1)


def conv_branch(feature, weight, scaling):
    number = feature.shape[0]
    channels = feature.shape[2]
    grouped = feature.reshape(number, GRID * GRID, GROUPS, channels // GROUPS)
    centre = jnp.mean(grouped, axis=(1, 3), keepdims=True)
    spread_sq = jnp.mean(jnp.square(grouped - centre), axis=(1, 3), keepdims=True)
    normed = ((grouped - centre) * lax.rsqrt(spread_sq + 1e-05)).reshape(
        number, GRID * GRID, channels
    )
    factor = scaling[:, None, :channels]
    offset = scaling[:, None, channels:]
    active = jax.nn.silu(normed * (1.0 + factor) + offset).astype(jnp.bfloat16)
    padded = jnp.pad(active.reshape(number, GRID, GRID, channels), ((0, 0), (1, 1), (1, 1), (0, 0)))
    taps = [
        padded[:, row_tap : row_tap + GRID, col_tap : col_tap + GRID, :]
        for row_tap in range(3)
        for col_tap in range(3)
    ]
    columns = jnp.concatenate(taps, axis=-1).reshape(number * GRID * GRID, 9 * channels)
    product = jnp.dot(columns, weight, preferred_element_type=jnp.float32)
    return product.reshape(number, GRID * GRID, channels)


def residual_block(feature, weight, scaling):
    primal = feature.astype(jnp.float32)
    return (primal + conv_branch(primal, weight, scaling)).astype(jnp.bfloat16)


def block_adjoint(feature, weight, scaling, upstream):
    primal = feature.astype(jnp.float32)

    def branch_only(probe):
        return conv_branch(probe, weight, scaling)

    _, pullback = jax.vjp(branch_only, primal)
    upstream_f = upstream.astype(jnp.float32)
    return (upstream_f + pullback(upstream_f)[0]).astype(jnp.bfloat16)


def section_total(partial_sum):
    return lax.psum(partial_sum.astype(jnp.bfloat16), "section").astype(jnp.float32)


def send_forward(value):
    return shifted(value, "section", 1)


def send_backward(value):
    return shifted(value, "section", -1)


def spread(value, owner):
    return from_root(value, "section", owner)


def store_one(buffer, value, index_at, is_live):
    previous = lax.dynamic_index_in_dim(buffer, index_at, 0, keepdims=False)
    return lax.dynamic_update_index_in_dim(buffer, jnp.where(is_live, value, previous), index_at, 0)


def run_chain(position, entering, worker, sender):
    number = entering.shape[0]
    clocks = number + lax.axis_size("section") - 1

    def advance(clock, state_in):
        incoming, sources, results = state_in
        member = clock - position
        is_live = (member >= 0) & (member < number)
        index_at = jnp.clip(member, 0, number - 1)
        entry_row = lax.dynamic_index_in_dim(entering, index_at, 0, keepdims=False)
        source = jnp.where(position == 0, entry_row, incoming)

        def run_work():
            return worker(source, index_at)

        def pass_through():
            return source

        result = lax.cond(is_live, run_work, pass_through)
        sources = store_one(sources, source, index_at, is_live)
        results = store_one(results, result, index_at, is_live)
        return (sender(result), sources, results)

    start = (jnp.zeros_like(entering[0]), jnp.zeros_like(entering), jnp.zeros_like(entering))
    final_state = lax.fori_loop(0, clocks, advance, start)
    return (final_state[1], final_state[2])


def local(
    images,
    noise_draw,
    cotangent,
    hue_angle,
    saturation,
    timestep,
    stem_weight,
    conv_weight,
    emb_weight,
    head_weight,
):
    sections = lax.axis_size("section")
    place = lax.axis_index("section")
    number = images.shape[0]
    columns_here = images.shape[2]
    full_conv = lax.all_gather(conv_weight, "batch", axis=1, tiled=True)[0]
    level = noise_levels(timestep)
    root_level = jnp.sqrt(level)[:, None, None]
    root_noise = jnp.sqrt(1.0 - level)[:, None, None]
    matrix, hue_slope, sat_slope = colour_maps(hue_angle, saturation)
    pixels = images.astype(jnp.float32).reshape(number, GRID * GRID, columns_here // 3, 3)
    coloured = apply_map(matrix, pixels).reshape(number, GRID * GRID, columns_here)
    noised = root_level * coloured + root_noise * noise_draw.astype(jnp.float32)
    entry_part = jnp.dot(
        noised.astype(jnp.bfloat16).reshape(-1, columns_here),
        stem_weight,
        preferred_element_type=jnp.float32,
    )
    first = section_total(entry_part).astype(jnp.bfloat16).reshape(number, GRID * GRID, CH)
    offsets = jnp.dot(time_features(timestep), emb_weight[0], preferred_element_type=jnp.float32)

    def forward_work(source, index_at):
        scaling = lax.dynamic_slice_in_dim(offsets, index_at, 1, 0)
        return residual_block(source[None], full_conv, scaling)[0]

    fwd_inputs, fwd_outputs = run_chain(place, first, forward_work, send_forward)
    finals = spread(fwd_outputs, sections - 1)
    predicted = jnp.dot(finals.reshape(-1, CH), head_weight, preferred_element_type=jnp.float32)
    predicted = predicted.reshape(number, GRID * GRID, columns_here)
    purified = ((noised - root_noise * predicted) / root_level).astype(jnp.bfloat16)
    weighted = cotangent.astype(jnp.float32) * (1.0 / math.sqrt(GRID * GRID * PV))
    eps_grad = (-(root_noise / root_level) * weighted).astype(jnp.bfloat16)
    seed_part = lax.dot_general(
        eps_grad.reshape(-1, columns_here),
        head_weight,
        (((1,), (1,)), ((), ())),
        preferred_element_type=jnp.float32,
    )
    seed = section_total(seed_part).astype(jnp.bfloat16).reshape(number, GRID * GRID, CH)

    def adjoint_work(source, index_at):
        saved = lax.dynamic_index_in_dim(fwd_inputs, index_at, 0, keepdims=True)
        scaling = lax.dynamic_slice_in_dim(offsets, index_at, 1, 0)
        return block_adjoint(saved, full_conv, scaling, source[None])[0]

    back_inputs, back_outputs = run_chain(sections - 1 - place, seed, adjoint_work, send_backward)
    grads = spread(back_outputs, 0)
    stem_back = lax.dot_general(
        grads.reshape(-1, CH),
        stem_weight,
        (((1,), (1,)), ((), ())),
        preferred_element_type=jnp.float32,
    )
    stem_back = stem_back.reshape(number, GRID * GRID, columns_here)
    pixel_grad = (weighted + root_level * stem_back).reshape(
        number, GRID * GRID, columns_here // 3, 3
    )
    hue_part = jnp.sum(pixel_grad * apply_map(hue_slope, pixels), axis=(1, 2, 3))
    sat_part = jnp.sum(pixel_grad * apply_map(sat_slope, pixels), axis=(1, 2, 3))
    colour_grad = section_total(jnp.stack([hue_part, sat_part], axis=1))
    return (purified, colour_grad)


def solution(mesh):
    in_specs = (
        P("batch", None, "section"),
        P("batch", None, "section"),
        P("batch", None, "section"),
        P("batch"),
        P("batch"),
        P("batch"),
        P("section", None),
        P("section", "batch", None),
        P("section", None, None),
        P(None, "section"),
    )
    out_specs = (P("batch", None, "section"), P("batch", None))
    return jax.shard_map(local, mesh=mesh, in_specs=in_specs, out_specs=out_specs, check_vma=False)
```

profile of v0, /device:TPU:0, one launch (start us, length us, event | category | flops | bytes accessed | tf_op | source)
XLA Modules:
  0.0 400.9 jit_solution(12375936215744181771)
XLA Ops:
  8.9 3.1 copy.20
  12.0 3.4 copy.21
  15.4 3.4 multiply_reduce_fusion.2
  18.9 3.3 copy.22
  22.2 3.4 copy.23
  26.4 1.6 fusion.82
  28.1 3.2 convolution_convert_fusion.2
  31.3 1.9 convolution_convert_fusion.1
  34.0 3.4 fusion.58
  37.4 27.4 %all-reduce.18.cloned.1.call-done = (bf16[2,64,1024]{2,1,0:T(8,128)(2,1)}, bf16[2,64,1024]{2,1,0:T(8,128)(2,1)}) async-done(((bf16[2,64,1024]{2,1,0:T(8,128)(2,1)}, bf16[2,64,1024]{2,1,0:T(8,128)(2,1)}), (bf16[2,64,1024]{2,1,0:T(8,128)(2,1)}, bf16[2,64,1024]{2,1,0:T(8,128)(2,1)})) %all-reduce.18.cloned.1.call-update) | async-done | bytes 524304 | tf_op jit(solution)/shard_map/psum | solution.py:101
  64.8 72.1 %all-gather.2.cloned.1.call-done = bf16[1,9216,1024]{2,1,0:T(8,128)(2,1)} async-done(((bf16[1,576,1024]{2,1,0:T(8,128)(2,1)}), bf16[1,9216,1024]{2,1,0:T(8,128)(2,1)}) %all-gather.2.cloned.1.call-update) | async-done | bytes 18874384 | tf_op jit(solution)/shard_map/all_gather | solution.py:165
  138.3 72.6 %while.34 = (s32[]{:T(128)}, bf16[64,1024]{1,0:T(8,128)(2,1)}, bf16[2,64,1024]{2,1,0:T(8,128)(2,1)S(1)}, bf16[2,64,1024]{2,1,0:T(8,128)(2,1)}, s32[]{:T(128)}, /...) while((s32[]{:T(128)}, bf16[64,1024]{1,0:T(8,128)(2,1)}, ...), condition=%wide.region_12.13_spmd, body=%wide.region_5.12_spmd.sunk | while | flops 1210057728 | bytes 25409360 | solution.py:145
  138.3 1.0 bitcast_dynamic-update-slice_fusion.6
  139.3 18.3 %conditional.4 = (bf16[64,1024]{1,0:T(8,128)(2,1)S(1)}) conditional(s32[]{:T(128)} %convert_element_type.245, bf16[64,1024]{1,0:T(8,128)(2,1)S(1)} %get-tuple-element.587, (bf16[64,1024]{1,0:T(8,128)(2,1)S(1)}, s32[]{:T(128)}, f32[2,2048]{1,0:T(2,128)}, bf16[9216,1024]{1,0:T(8,128)(2,1)}) %tuple.116), branch_computations={%region_6.6_spmd, %region_7.11_spmd} | conditional | flops 1209861120 | bytes 23311430 | solution.py:139
  147.8 9.8 %fusion = bf16[64,1024]{1,0:T(8,128)(2,1)S(1)} fusion(bf16[64,9216]{1,0:T(8,128)(2,1)S(1)} %fusion.32, bf16[9216,1024]{1,0:T(8,128)(2,1)} %get-tuple-element.369, bf16[64,1024]{1,0:T(8,128)(2,1)S(1)} %get-tuple-element.366), kind=kOutput, calls=%fused_computation.1 | convolution fusion | flops 1208156160 | bytes 20316160 | tf_op jit(solution)/shard_map/while/body/eval_jaxpr/cond/branch_1_fun/dot_general | solution.py:80
  157.7 0.9 constant_dynamic-slice_fusion.7
  159.3 4.1 %collective-permute-done = bf16[64,1024]{1,0:T(8,128)(2,1)} collective-permute-done((bf16[64,1024]{1,0:T(8,128)(2,1)S(1)}, bf16[64,1024]{1,0:T(8,128)(2,1)}, u32[]{:S(2)}, u32[]{:S(2)}) %collective-permute-start) | collective-permute-done | bytes 131104 | tf_op jit(solution)/shard_map/while/body/eval_jaxpr/ppermute | solution.py:18
  163.5 1.0 bitcast_dynamic-update-slice_fusion.6
  164.5 18.3 %conditional.4 = (bf16[64,1024]{1,0:T(8,128)(2,1)S(1)}) conditional(s32[]{:T(128)} %convert_element_type.245, bf16[64,1024]{1,0:T(8,128)(2,1)S(1)} %get-tuple-element.587, (bf16[64,1024]{1,0:T(8,128)(2,1)S(1)}, s32[]{:T(128)}, f32[2,2048]{1,0:T(2,128)}, bf16[9216,1024]{1,0:T(8,128)(2,1)}) %tuple.116), branch_computations={%region_6.6_spmd, %region_7.11_spmd} | conditional | flops 1209861120 | bytes 23311430 | solution.py:139
  172.9 9.8 %fusion = bf16[64,1024]{1,0:T(8,128)(2,1)S(1)} fusion(bf16[64,9216]{1,0:T(8,128)(2,1)S(1)} %fusion.32, bf16[9216,1024]{1,0:T(8,128)(2,1)} %get-tuple-element.369, bf16[64,1024]{1,0:T(8,128)(2,1)S(1)} %get-tuple-element.366), kind=kOutput, calls=%fused_computation.1 | convolution fusion | flops 1208156160 | bytes 20316160 | tf_op jit(solution)/shard_map/while/body/eval_jaxpr/cond/branch_1_fun/dot_general | solution.py:80
  183.2 0.9 constant_dynamic-slice_fusion.7
  184.8 3.1 collective-permute-done
  187.9 1.0 bitcast_dynamic-update-slice_fusion.6
  188.9 19.0 %collective-permute-start = (bf16[64,1024]{1,0:T(8,128)(2,1)S(1)}, bf16[64,1024]{1,0:T(8,128)(2,1)}, u32[]{:S(2)}, u32[]{:S(2)}) collective-permute-start(bf16[64,1024]{1,0:T(8,128)(2,1)S(1)} %get-tuple-element.674), channel_id=1, source_target_pairs={{0,16},{16,0},{1,17},{17,1},{2,18},{18,2},{3,19},{19,3},{4,20},{20... | collective-permute-start | bytes 393224 | tf_op jit(solution)/shard_map/while/body/eval_jaxpr/ppermute | solution.py:18
  207.9 0.9 constant_dynamic-slice_fusion.7
  209.5 1.5 collective-permute-done
  212.3 138.6 %while.35 = (s32[]{:T(128)}, bf16[64,1024]{1,0:T(8,128)(2,1)}, bf16[2,64,1024]{2,1,0:T(8,128)(2,1)}, s32[]{:T(128)}, pred[]{:T(512)}, /*index=5*/bf16[2,64,1024]...) while((s32[]{:T(128)}, bf16[64,1024]{1,0:T(8,128)(2,1)}, ...), condition=%wide.region_28.29_spmd, body=%wide.region_15.28_spmd.sunk | while | flops 1212769664 | bytes 27270924 | solution.py:145
  212.3 1.0 bitcast_select_fusion.7
  213.3 42.1 %collective-permute-start.1 = (bf16[64,1024]{1,0:T(8,128)(2,1)S(1)}, bf16[64,1024]{1,0:T(8,128)(2,1)}, u32[]{:S(2)}, u32[]{:S(2)}) collective-permute-start(bf16[64,1024]{1,0:T(8,128)(2,1)S(1)} %get-tuple-element.675), channel_id=1, source_target_pairs={{0,16},{16,0},{1,17},{17,1},{2,18},{18,2},{3,19},{19,3},{4,20},{20... | collective-permute-start | bytes 393224 | tf_op jit(solution)/shard_map/while/body/eval_jaxpr/ppermute | solution.py:18
  255.4 0.9 constant_dynamic-slice_fusion.8
  257.0 1.4 collective-permute-done.1
  258.5 1.0 bitcast_select_fusion.7
  259.5 40.1 %conditional.5 = (bf16[64,1024]{1,0:T(8,128)(2,1)S(1)}) conditional(s32[]{:T(128)} %convert_element_type.246, bf16[64,1024]{1,0:T(8,128)(2,1)S(1)} %bitcast_select_fusion.7, (bf16[64,1024]{1,0:T(8,128)(2,1)S(1)}, bf16[9216,1024]{1,0:T(8,128)(2,1)}, s32[]{:T(128)}, bf16[2,64,1024]{2,1,0:T(8,128)(2,1)S(1)}, f32[2,2048]{1,0:T(2,128)}) %tuple.118), branch_computations={%region_16.16_spmd, %region_17.27_spmd} | conditional | flops 1212638592 | bytes 25697282 | solution.py:139
  267.2 13.2 %fusion.33 = bf16[1,8,8,9216]{3,2,1,0:T(8,128)(2,1)} fusion(bf16[64,1024]{1,0:T(8,128)(2,1)S(1)} %get-tuple-element.380, bf16[9216,1024]{1,0:T(8,128)(2,1)} %get-tuple-element.381), kind=kOutput, calls=%fused_computation.57 | convolution fusion | flops 1208549376 | bytes 20185088 | tf_op jit(solution)/shard_map/while/body/eval_jaxpr/cond/branch_1_fun/transpose(jvp())/dot_general | solution.py:80
  280.4 2.2 fusion.94
  282.6 0.9 pad_add_fusion
  284.3 3.0 multiply_reduce_fusion
  287.2 1.3 reduce_sum.142
  292.2 1.4 reduce_sum.154
  293.5 1.4 reduce_sum.155
  298.5 1.1 fusion.55
  299.6 2.0 collective-permute-start.1
  301.6 0.9 constant_dynamic-slice_fusion.8
  303.2 1.5 collective-permute-done.1
  304.7 1.0 bitcast_select_fusion.7
  305.7 40.1 %conditional.5 = (bf16[64,1024]{1,0:T(8,128)(2,1)S(1)}) conditional(s32[]{:T(128)} %convert_element_type.246, bf16[64,1024]{1,0:T(8,128)(2,1)S(1)} %bitcast_select_fusion.7, (bf16[64,1024]{1,0:T(8,128)(2,1)S(1)}, bf16[9216,1024]{1,0:T(8,128)(2,1)}, s32[]{:T(128)}, bf16[2,64,1024]{2,1,0:T(8,128)(2,1)S(1)}, f32[2,2048]{1,0:T(2,128)}) %tuple.118), branch_computations={%region_16.16_spmd, %region_17.27_spmd} | conditional | flops 1212638592 | bytes 25697282 | solution.py:139
  313.4 13.2 %fusion.33 = bf16[1,8,8,9216]{3,2,1,0:T(8,128)(2,1)} fusion(bf16[64,1024]{1,0:T(8,128)(2,1)S(1)} %get-tuple-element.380, bf16[9216,1024]{1,0:T(8,128)(2,1)} %get-tuple-element.381), kind=kOutput, calls=%fused_computation.57 | convolution fusion | flops 1208549376 | bytes 20185088 | tf_op jit(solution)/shard_map/while/body/eval_jaxpr/cond/branch_1_fun/transpose(jvp())/dot_general | solution.py:80
  326.6 2.2 fusion.94
  330.5 3.0 multiply_reduce_fusion
  333.5 1.3 reduce_sum.142
  338.4 1.4 reduce_sum.154
  339.7 1.4 reduce_sum.155
  344.7 1.1 fusion.55
  345.9 0.9 constant_dynamic-slice_fusion.8
  347.5 3.4 collective-permute-done.1
  350.9 1.7 broadcast_select_fusion
  353.3 3.3 copy.24
  356.6 3.4 copy.25
  360.0 3.3 copy.26
  363.3 3.4 copy.27
  366.7 14.6 %all-reduce.16.cloned.1.call-done = (bf16[2,64,1024]{2,1,0:T(8,128)(2,1)}, bf16[2,64,1024]{2,1,0:T(8,128)(2,1)}) async-done(((bf16[2,64,1024]{2,1,0:T(8,128)(2,1)}, bf16[2,64,1024]{2,1,0:T(8,128)(2,1)}), (bf16[2,64,1024]{2,1,0:T(8,128)(2,1)}, bf16[2,64,1024]{2,1,0:T(8,128)(2,1)})) %all-reduce.16.cloned.1.call-update) | async-done | bytes 524304 | tf_op jit(solution)/shard_map/psum | solution.py:23
  381.4 3.8 multiply_reduce_fusion.5
  385.2 4.9 %psum.39 = bf16[2,2]{0,1:T(2,128)(2,1)S(1)} all-reduce(bf16[2,2]{0,1:T(2,128)(2,1)S(1)} %pad_maximum_fusion.1), channel_id=1, replica_groups=mesh['section'=2,'batch'=16] {'section'}, use_global_device_ids=true, to_apply=%region_34.35 | all-reduce | flops 4 | bytes 16 | tf_op jit(solution)/shard_map/psum | solution.py:101
  390.8 2.7 fusion.79
  (157 shorter events, 60.5 us)
Async XLA Ops:
  8.0 23.3 %copy-start = (bf16[1024,1536]{1,0:T(8,128)(2,1)S(1)}, bf16[1024,1536]{1,0:T(8,128)(2,1)}, u32[]{:S(2)}) copy-start(bf16[1024,1536]{1,0:T(8,128)(2,1)} %param.28) | copy-start | bytes 9437188
  8.0 56.8 %all-reduce.18.cloned.1.call-start = ((), (), s32[]{:S(2)}) async-start(), calls=%async_computation.2 | async-start | bytes 1048576 | tf_op jit(solution)/shard_map/psum | solution.py:101
  12.0 3.4 copy-start.6
  12.0 3.4 copy-start.7
  22.2 4.0 %copy-start.8 = (s32[2]{0:T(128)S(1)}, s32[2]{0:T(128)}, u32[]{:S(2)}) copy-start(s32[2]{0:T(128)} %param.24) | copy-start | bytes 28
  26.4 4.8 %copy-start.2 = (f32[2]{0:T(128)}, f32[2]{0:T(128)S(1)}, u32[]{:S(2)}) copy-start(f32[2]{0:T(128)S(1)} %get-tuple-element.477) | copy-start | bytes 28
  26.4 4.8 %copy-start.4 = (f32[2]{0:T(128)}, f32[2]{0:T(128)S(1)}, u32[]{:S(2)}) copy-start(f32[2]{0:T(128)S(1)} %get-tuple-element.479) | copy-start | bytes 28
  33.1 103.8 %all-gather.2.cloned.1.call-start = ((), (), s32[]{:S(2)}) async-start(), calls=%async_computation | async-start | bytes 20054016 | tf_op jit(solution)/shard_map/all_gather | solution.py:165
  33.7 347.6 %all-reduce.16.cloned.1.call-start = ((), (), s32[]{:S(2)}) async-start(), calls=%async_computation.1 | async-start | bytes 1048576 | tf_op jit(solution)/shard_map/psum | solution.py:23
  157.6 5.8 %collective-permute-start = (bf16[64,1024]{1,0:T(8,128)(2,1)S(1)}, bf16[64,1024]{1,0:T(8,128)(2,1)}, u32[]{:S(2)}, u32[]{:S(2)}) collective-permute-start(bf16[64,1024]{1,0:T(8,128)(2,1)S(1)} %get-tuple-element.674), channel_id=1, source_target_pairs={{0,16},{16,0},{1,17},{17,1},{2,18},{18,2},{3,19},{19,3},{4,20},{20... | collective-permute-start | bytes 393224 | tf_op jit(solution)/shard_map/while/body/eval_jaxpr/ppermute | solution.py:18
  182.8 5.1 %collective-permute-start = (bf16[64,1024]{1,0:T(8,128)(2,1)S(1)}, bf16[64,1024]{1,0:T(8,128)(2,1)}, u32[]{:S(2)}, u32[]{:S(2)}) collective-permute-start(bf16[64,1024]{1,0:T(8,128)(2,1)S(1)} %get-tuple-element.674), channel_id=1, source_target_pairs={{0,16},{16,0},{1,17},{17,1},{2,18},{18,2},{3,19},{19,3},{4,20},{20... | collective-permute-start | bytes 393224 | tf_op jit(solution)/shard_map/while/body/eval_jaxpr/ppermute | solution.py:18
  188.9 22.0 %collective-permute-start = (bf16[64,1024]{1,0:T(8,128)(2,1)S(1)}, bf16[64,1024]{1,0:T(8,128)(2,1)}, u32[]{:S(2)}, u32[]{:S(2)}) collective-permute-start(bf16[64,1024]{1,0:T(8,128)(2,1)S(1)} %get-tuple-element.674), channel_id=1, source_target_pairs={{0,16},{16,0},{1,17},{17,1},{2,18},{18,2},{3,19},{19,3},{4,20},{20... | collective-permute-start | bytes 393224 | tf_op jit(solution)/shard_map/while/body/eval_jaxpr/ppermute | solution.py:18
  213.3 45.2 %collective-permute-start.1 = (bf16[64,1024]{1,0:T(8,128)(2,1)S(1)}, bf16[64,1024]{1,0:T(8,128)(2,1)}, u32[]{:S(2)}, u32[]{:S(2)}) collective-permute-start(bf16[64,1024]{1,0:T(8,128)(2,1)S(1)} %get-tuple-element.675), channel_id=1, source_target_pairs={{0,16},{16,0},{1,17},{17,1},{2,18},{18,2},{3,19},{19,3},{4,20},{20... | collective-permute-start | bytes 393224 | tf_op jit(solution)/shard_map/while/body/eval_jaxpr/ppermute | solution.py:18
  265.2 0.5 copy-start.1
  299.6 5.1 %collective-permute-start.1 = (bf16[64,1024]{1,0:T(8,128)(2,1)S(1)}, bf16[64,1024]{1,0:T(8,128)(2,1)}, u32[]{:S(2)}, u32[]{:S(2)}) collective-permute-start(bf16[64,1024]{1,0:T(8,128)(2,1)S(1)} %get-tuple-element.675), channel_id=1, source_target_pairs={{0,16},{16,0},{1,17},{17,1},{2,18},{18,2},{3,19},{19,3},{4,20},{20... | collective-permute-start | bytes 393224 | tf_op jit(solution)/shard_map/while/body/eval_jaxpr/ppermute | solution.py:18
  311.4 0.5 copy-start.1
  345.8 5.1 %collective-permute-start.1 = (bf16[64,1024]{1,0:T(8,128)(2,1)S(1)}, bf16[64,1024]{1,0:T(8,128)(2,1)}, u32[]{:S(2)}, u32[]{:S(2)}) collective-permute-start(bf16[64,1024]{1,0:T(8,128)(2,1)S(1)} %get-tuple-element.675), channel_id=1, source_target_pairs={{0,16},{16,0},{1,17},{17,1},{2,18},{18,2},{3,19},{19,3},{4,20},{20... | collective-permute-start | bytes 393224 | tf_op jit(solution)/shard_map/while/body/eval_jaxpr/ppermute | solution.py:18
  363.3 18.0 %copy-start.3 = (f32[2]{0:T(128)S(1)}, f32[2]{0:T(128)}, u32[]{:S(2)}) copy-start(f32[2]{0:T(128)} %copy-done.2) | copy-start | bytes 28
  381.4 9.4 %copy-start.5 = (f32[2]{0:T(128)S(1)}, f32[2]{0:T(128)}, u32[]{:S(2)}) copy-start(f32[2]{0:T(128)} %copy-done.4) | copy-start | bytes 28
Sparse Core Ops, SparseCore 0:
  33.3 31.5 all-reduce.17
  353.5 27.8 all-reduce.15
Sparse Core Ops, SparseCore 1:
  35.3 101.6 all-gather.1
where the time goes:
time: 404 us; the launch traced here: 401 us
  waiting for transfers between devices  130 us (32%)
  local copies, waits for them, and re-layouts  72.5 us (18%)
  starting transfers between devices  63.8 us (16%)
  matrix products  61.1 us (15%)
  other arithmetic  52.8 us (13%)
  between operations  15.6 us (4%)
  blocking collectives  4.94 us (1%)
    all_gather x1, waiting for transfers between devices, local(): full_conv = lax.all_gather(conv_weight, 'batch', axis=1, tiled=True)[0]  72.1 us
    ppermute x6, starting transfers between devices, shifted(): return lax.ppermute(value, axis, pairs)  63.6 us
    dot_general x4, matrix products, conv_branch(): product = jnp.dot(columns, weight, preferred_element_type=jnp.float32)  46.1 us
    psum x1, waiting for transfers between devices, section_total(): lax.psum(partial_sum.astype(jnp.bfloat16), 'section').astype(jnp.float32)  27.4 us
    reduce_sum x5, local copies, waits for them, and re-layouts, apply_map(): jnp.sum(matrix[:, None, None, :, :] * pixels[:, :, :, None, :], axis=-1)  16.7 us
    ppermute x6, waiting for transfers between devices, shifted(): return lax.ppermute(value, axis, pairs)  15.1 us
    psum x1, waiting for transfers between devices, from_root(): return lax.psum(block, axis)  14.6 us
    reduce_sum x8, other arithmetic, conv_branch(): grouped - centre  11.6 us
  transfers between devices with their start and end apart: 9, of which 9 were waited for; matrix products, arithmetic and copies ran while one was open for 7% of the time, Pallas kernels for 0%

commit v1 on v0

--- a/solution.py
+++ b/solution.py
@@ -10,6 +10,24 @@
 GRID = 8
 TSTEPS = 1000
 PV = 3072
+
+
+def ring_gather(array, axis, dim):
+    ways, here, step = (lax.axis_size(axis), lax.axis_index(axis), array.shape[dim])
+    shape = [n * ways if d == dim else n for d, n in enumerate(array.shape)]
+    full = lax.dynamic_update_slice_in_dim(
+        jnp.zeros(shape, array.dtype), array, here * step, axis=dim
+    )
+    going_up = going_down = array
+    for far in range(1, ways // 2 + 1):
+        going_up = lax.ppermute(going_up, axis, [(d, (d + 1) % ways) for d in range(ways)])
+        full = lax.dynamic_update_slice_in_dim(full, going_up, (here - far) % ways * step, axis=dim)
+        if 2 * far < ways:
+            going_down = lax.ppermute(going_down, axis, [(d, (d - 1) % ways) for d in range(ways)])
+            full = lax.dynamic_update_slice_in_dim(
+                full, going_down, (here + far) % ways * step, axis=dim
+            )
+    return full
 
 
 def shifted(value, axis, steps):
@@ -162,7 +180,7 @@
     place = lax.axis_index("section")
     number = images.shape[0]
     columns_here = images.shape[2]
-    full_conv = lax.all_gather(conv_weight, "batch", axis=1, tiled=True)[0]
+    full_conv = ring_gather(conv_weight, "batch", 1)[0]
     level = noise_levels(timestep)
     root_level = jnp.sqrt(level)[:, None, None]
     root_noise = jnp.sqrt(1.0 - level)[:, None, None]

time: 404 us -> 491 us (1.22)
  starting transfers between devices: 63.8 us -> 172 us
  waiting for transfers between devices: 130 us -> 70.8 us
  local copies, waits for them, and re-layouts: 72.5 us -> 111 us
    ppermute x0 -> x15, starting transfers between devices: none -> 109 us  [the longest x8 99.2 us: ring_gather(): lax.ppermute(going_up, axis, [(d, (d + 1) % ways) for d in range(ways)])]
    all_gather x1 -> x0, waiting for transfers between devices: 72.1 us -> none  [local(): full_conv = lax.all_gather(conv_weight, 'batch', axis=1, tiled=True)[0]]
    ppermute x0 -> x15, waiting for transfers between devices: none -> 32 us  [the longest x8 32 us: ring_gather(): lax.ppermute(going_up, axis, [(d, (d + 1) % ways) for d in range(ways)])]
    dynamic_update_slice x0 -> x16, local copies, waits for them, and re-layouts: none -> 31.9 us  [the longest x8 16.6 us: ring_gather(): lax.dynamic_update_slice_in_dim(full, going_up, (here - far) % ways * ste...]
    psum x1, waiting for transfers between devices: 27.4 us -> 0.01 us  [section_total(): lax.psum(partial_sum.astype(jnp.bfloat16), 'section').astype(jnp.float32)]
    psum x1, waiting for transfers between devices: 14.6 us -> 24 us  [from_root(): return lax.psum(block, axis)]
    squeeze x0 -> x1, local copies, waits for them, and re-layouts: none -> 6.74 us  [local(): full_conv = ring_gather(conv_weight, 'batch', 1)[0]]
  transfers between devices with their start and end apart: 9 -> 23, of which waited for: 9 -> 11; matrix products, arithmetic and copies ran while one was open for 7% -> 18% of each run, Pallas kernels for 0% -> 0%
where the time goes in v1:
time: 491 us; the launch traced here: 488 us
  starting transfers between devices  172 us (35%)
  local copies, waits for them, and re-layouts  111 us (23%)
  waiting for transfers between devices  70.8 us (14%)
  matrix products  61 us (12%)
  other arithmetic  53.5 us (11%)
  between operations  14.2 us (3%)
  blocking collectives  4.94 us (1%)
    ppermute x8, starting transfers between devices, ring_gather(): lax.ppermute(going_up, axis, [(d, (d + 1) % ways) for d in range(ways)])  99.2 us
    ppermute x6, starting transfers between devices, shifted(): return lax.ppermute(value, axis, pairs)  62.9 us
    dot_general x4, matrix products, conv_branch(): product = jnp.dot(columns, weight, preferred_element_type=jnp.float32)  46.1 us
    ppermute x8, waiting for transfers between devices, ring_gather(): lax.ppermute(going_up, axis, [(d, (d + 1) % ways) for d in range(ways)])  32 us
    psum x1, waiting for transfers between devices, from_root(): return lax.psum(block, axis)  24 us
    reduce_sum x5, local copies, waits for them, and re-layouts, apply_map(): jnp.sum(matrix[:, None, None, :, :] * pixels[:, :, :, None, :], axis=-1)  16.8 us
    dynamic_update_slice x8, local copies, waits for them, and re-layouts, ring_gather(): lax.dynamic_update_slice_in_dim(full, going_up, (here - far) % ways * ste...  16.6 us
    ppermute x6, waiting for transfers between devices, shifted(): return lax.ppermute(value, axis, pairs)  14.7 us
  transfers between devices with their start and end apart: 23, of which 11 were waited for; matrix products, arithmetic and copies ran while one was open for 18% of the time, Pallas kernels for 0%

profile of v1, /device:TPU:0, one launch (start us, length us, event | category | flops | bytes accessed | tf_op | source)
XLA Modules:
  0.0 487.9 jit_solution(17865519318619300279)
XLA Ops:
  7.8 5.0 %collective-permute-start.3 = (bf16[1,576,1024]{2,1,0:T(8,128)(2,1)}, bf16[1,576,1024]{2,1,0:T(8,128)(2,1)}, u32[]{:S(2)}, u32[]{:S(2)}) collective-permute-start(bf16[1,576,1024]{2,1,0:T(8,128)(2,1)} %param.26), channel_id=1, source_target_pairs={{0,15},{1,0},{2,1},{3,2},{4,3},{5,4},{6,5},{7,6},{8,7},{9,8},{10,9... | collective-permute-start | bytes 3538952 | tf_op jit(solution)/shard_map/ppermute | solution.py:26
  12.8 14.1 %collective-permute-done.2 = bf16[1,576,1024]{2,1,0:T(8,128)(2,1)S(1)} collective-permute-done((bf16[1,576,1024]{2,1,0:T(8,128)(2,1)}, bf16[1,576,1024]{2,1,0:T(8,128)(2,1)S(1)}, u32[]{:S(2)}, u32[]{:S(2)}) %collective-permute-start.2) | collective-permute-done | bytes 1179680 | tf_op jit(solution)/shard_map/ppermute | solution.py:23
  28.0 9.5 %collective-permute-start.4 = (bf16[1,576,1024]{2,1,0:T(8,128)(2,1)S(1)}, bf16[1,576,1024]{2,1,0:T(8,128)(2,1)}, u32[]{:S(2)}, u32[]{:S(2)}) collective-permute-start(bf16[1,576,1024]{2,1,0:T(8,128)(2,1)S(1)} %collective-permute-done.2), channel_id=1, source_target_pairs={{0,1},{1,2},{2,3},{3,4},{4,5},{5,6},{6,7},{7,8},{8,9},{9,10},{10,1... | collective-permute-start | bytes 3538952 | tf_op jit(solution)/shard_map/ppermute | solution.py:23
  37.5 9.0 %collective-permute-done.4 = bf16[1,576,1024]{2,1,0:T(8,128)(2,1)} collective-permute-done((bf16[1,576,1024]{2,1,0:T(8,128)(2,1)S(1)}, bf16[1,576,1024]{2,1,0:T(8,128)(2,1)}, u32[]{:S(2)}, u32[]{:S(2)}) %collective-permute-start.4) | collective-permute-done | bytes 1179680 | tf_op jit(solution)/shard_map/ppermute | solution.py:23
  46.5 18.7 %collective-permute-start.6 = (bf16[1,576,1024]{2,1,0:T(8,128)(2,1)}, bf16[1,576,1024]{2,1,0:T(8,128)(2,1)}, u32[]{:S(2)}, u32[]{:S(2)}) collective-permute-start(bf16[1,576,1024]{2,1,0:T(8,128)(2,1)} %collective-permute-done.4), channel_id=1, source_target_pairs={{0,1},{1,2},{2,3},{3,4},{4,5},{5,6},{6,7},{7,8},{8,9},{9,10},{10,1... | collective-permute-start | bytes 3538952 | tf_op jit(solution)/shard_map/ppermute | solution.py:23
  65.2 3.0 copy.20
  68.2 3.4 copy.21
  71.8 3.5 multiply_reduce_fusion.2
  75.3 3.3 copy.22
  78.6 3.4 copy.23
  82.5 11.4 %collective-permute-start.8 = (bf16[1,576,1024]{2,1,0:T(8,128)(2,1)}, bf16[1,576,1024]{2,1,0:T(8,128)(2,1)}, u32[]{:S(2)}, u32[]{:S(2)}) collective-permute-start(bf16[1,576,1024]{2,1,0:T(8,128)(2,1)} %collective-permute-done.6), channel_id=1, source_target_pairs={{0,1},{1,2},{2,3},{3,4},{4,5},{5,6},{6,7},{7,8},{8,9},{9,10},{10,1... | collective-permute-start | bytes 3538952 | tf_op jit(solution)/shard_map/ppermute | solution.py:23
  95.1 1.5 fusion.82
  96.6 8.4 %collective-permute-done.8 = bf16[1,576,1024]{2,1,0:T(8,128)(2,1)} collective-permute-done((bf16[1,576,1024]{2,1,0:T(8,128)(2,1)}, bf16[1,576,1024]{2,1,0:T(8,128)(2,1)}, u32[]{:S(2)}, u32[]{:S(2)}) %collective-permute-start.8) | collective-permute-done | bytes 1179680 | tf_op jit(solution)/shard_map/ppermute | solution.py:23
  105.0 17.5 %collective-permute-start.10 = (bf16[1,576,1024]{2,1,0:T(8,128)(2,1)}, bf16[1,576,1024]{2,1,0:T(8,128)(2,1)}, u32[]{:S(2)}, u32[]{:S(2)}) collective-permute-start(bf16[1,576,1024]{2,1,0:T(8,128)(2,1)} %collective-permute-done.8), channel_id=1, source_target_pairs={{0,1},{1,2},{2,3},{3,4},{4,5},{5,6},{6,7},{7,8},{8,9},{9,10},{10,1... | collective-permute-start | bytes 3538952 | tf_op jit(solution)/shard_map/ppermute | solution.py:23
  122.5 3.2 convolution_convert_fusion.2
  125.7 1.8 convolution_convert_fusion.1
  127.9 3.4 fusion.58
  131.3 19.8 %collective-permute-start.12 = (bf16[1,576,1024]{2,1,0:T(8,128)(2,1)}, bf16[1,576,1024]{2,1,0:T(8,128)(2,1)}, u32[]{:S(2)}, u32[]{:S(2)}) collective-permute-start(bf16[1,576,1024]{2,1,0:T(8,128)(2,1)} %collective-permute-done.10), channel_id=1, source_target_pairs={{0,1},{1,2},{2,3},{3,4},{4,5},{5,6},{6,7},{7,8},{8,9},{9,10},{10,1... | collective-permute-start | bytes 3538952 | tf_op jit(solution)/shard_map/ppermute | solution.py:23
  151.1 6.7 %squeeze.82 = bf16[9216,1024]{1,0:T(8,128)(2,1)} broadcast(bf16[]{:T(256)} %constant.279.clone.1), dimensions={} | broadcast | bytes 18874370 | tf_op jit(solution)/shard_map/squeeze | solution.py:183
  158.9 2.4 bitcast_dynamic-update-slice_fusion.17
  161.3 2.4 bitcast_dynamic-update-slice_fusion.16
  163.7 2.4 bitcast_dynamic-update-slice_fusion.15
  166.1 2.4 bitcast_dynamic-update-slice_fusion.14
  168.5 2.4 collective-permute-start.14
  170.9 2.4 bitcast_dynamic-update-slice_fusion.13
  173.3 2.3 bitcast_dynamic-update-slice_fusion.12
  175.7 2.4 bitcast_dynamic-update-slice_fusion.11
  178.1 2.4 bitcast_dynamic-update-slice_fusion.10
  180.5 4.3 collective-permute-start.15
  184.8 2.4 bitcast_dynamic-update-slice_fusion.9
  187.2 19.3 %collective-permute-start.16 = (bf16[1,576,1024]{2,1,0:T(8,128)(2,1)S(1)}, bf16[1,576,1024]{2,1,0:T(8,128)(2,1)S(1)}, u32[]{:S(2)}, u32[]{:S(2)}) collective-permute-start(bf16[1,576,1024]{2,1,0:T(8,128)(2,1)S(1)} %collective-permute-done.14), channel_id=1, source_target_pairs={{0,1},{1,2},{2,3},{3,4},{4,5},{5,6},{6,7},{7,8},{8,9},{9,10},{10,1... | collective-permute-start | bytes 3538952 | tf_op jit(solution)/shard_map/ppermute | solution.py:23
  206.5 2.4 bitcast_dynamic-update-slice_fusion.8
  208.9 2.4 bitcast_dynamic-update-slice_fusion.7
  217.6 71.4 %while.34 = (s32[]{:T(128)}, bf16[64,1024]{1,0:T(8,128)(2,1)}, bf16[2,64,1024]{2,1,0:T(8,128)(2,1)S(1)}, bf16[2,64,1024]{2,1,0:T(8,128)(2,1)}, s32[]{:T(128)}, /...) while((s32[]{:T(128)}, bf16[64,1024]{1,0:T(8,128)(2,1)}, ...), condition=%wide.region_12.13_spmd, body=%wide.region_5.12_spmd.sunk | while | flops 1210057728 | bytes 25409360 | solution.py:163
  218.6 18.3 %conditional.4 = (bf16[64,1024]{1,0:T(8,128)(2,1)S(1)}) conditional(s32[]{:T(128)} %convert_element_type.245, bf16[64,1024]{1,0:T(8,128)(2,1)S(1)} %get-tuple-element.587, (bf16[64,1024]{1,0:T(8,128)(2,1)S(1)}, s32[]{:T(128)}, f32[2,2048]{1,0:T(2,128)}, bf16[9216,1024]{1,0:T(8,128)(2,1)}) %tuple.116), branch_computations={%region_6.6_spmd, %region_7.11_spmd} | conditional | flops 1209861120 | bytes 23311430 | solution.py:157
  227.1 9.8 %fusion = bf16[64,1024]{1,0:T(8,128)(2,1)S(1)} fusion(bf16[64,9216]{1,0:T(8,128)(2,1)S(1)} %fusion.32, bf16[9216,1024]{1,0:T(8,128)(2,1)} %get-tuple-element.369, bf16[64,1024]{1,0:T(8,128)(2,1)S(1)} %get-tuple-element.366), kind=kOutput, calls=%fused_computation.1 | convolution fusion | flops 1208156160 | bytes 20316160 | tf_op jit(solution)/shard_map/while/body/eval_jaxpr/cond/branch_1_fun/dot_general | solution.py:98
  238.6 3.4 collective-permute-done
  243.0 18.3 %conditional.4 = (bf16[64,1024]{1,0:T(8,128)(2,1)S(1)}) conditional(s32[]{:T(128)} %convert_element_type.245, bf16[64,1024]{1,0:T(8,128)(2,1)S(1)} %get-tuple-element.587, (bf16[64,1024]{1,0:T(8,128)(2,1)S(1)}, s32[]{:T(128)}, f32[2,2048]{1,0:T(2,128)}, bf16[9216,1024]{1,0:T(8,128)(2,1)}) %tuple.116), branch_computations={%region_6.6_spmd, %region_7.11_spmd} | conditional | flops 1209861120 | bytes 23311430 | solution.py:157
  251.5 9.8 %fusion = bf16[64,1024]{1,0:T(8,128)(2,1)S(1)} fusion(bf16[64,9216]{1,0:T(8,128)(2,1)S(1)} %fusion.32, bf16[9216,1024]{1,0:T(8,128)(2,1)} %get-tuple-element.369, bf16[64,1024]{1,0:T(8,128)(2,1)S(1)} %get-tuple-element.366), kind=kOutput, calls=%fused_computation.1 | convolution fusion | flops 1208156160 | bytes 20316160 | tf_op jit(solution)/shard_map/while/body/eval_jaxpr/cond/branch_1_fun/dot_general | solution.py:98
  263.1 3.4 collective-permute-done
  267.5 18.5 %collective-permute-start = (bf16[64,1024]{1,0:T(8,128)(2,1)S(1)}, bf16[64,1024]{1,0:T(8,128)(2,1)}, u32[]{:S(2)}, u32[]{:S(2)}) collective-permute-start(bf16[64,1024]{1,0:T(8,128)(2,1)S(1)} %get-tuple-element.674), channel_id=1, source_target_pairs={{0,16},{16,0},{1,17},{17,1},{2,18},{18,2},{3,19},{19,3},{4,20},{20... | collective-permute-start | bytes 393224 | tf_op jit(solution)/shard_map/while/body/eval_jaxpr/ppermute | solution.py:36
  290.4 138.8 %while.35 = (s32[]{:T(128)}, bf16[64,1024]{1,0:T(8,128)(2,1)}, bf16[2,64,1024]{2,1,0:T(8,128)(2,1)}, s32[]{:T(128)}, pred[]{:T(512)}, /*index=5*/bf16[2,64,1024]...) while((s32[]{:T(128)}, bf16[64,1024]{1,0:T(8,128)(2,1)}, ...), condition=%wide.region_28.29_spmd, body=%wide.region_15.28_spmd.sunk | while | flops 1212769664 | bytes 27270924 | solution.py:163
  291.4 42.2 %collective-permute-start.1 = (bf16[64,1024]{1,0:T(8,128)(2,1)S(1)}, bf16[64,1024]{1,0:T(8,128)(2,1)}, u32[]{:S(2)}, u32[]{:S(2)}) collective-permute-start(bf16[64,1024]{1,0:T(8,128)(2,1)S(1)} %get-tuple-element.675), channel_id=1, source_target_pairs={{0,16},{16,0},{1,17},{17,1},{2,18},{18,2},{3,19},{19,3},{4,20},{20... | collective-permute-start | bytes 393224 | tf_op jit(solution)/shard_map/while/body/eval_jaxpr/ppermute | solution.py:36
  335.2 1.5 collective-permute-done.1
  337.6 40.2 %conditional.5 = (bf16[64,1024]{1,0:T(8,128)(2,1)S(1)}) conditional(s32[]{:T(128)} %convert_element_type.246, bf16[64,1024]{1,0:T(8,128)(2,1)S(1)} %bitcast_select_fusion.7, (bf16[64,1024]{1,0:T(8,128)(2,1)S(1)}, bf16[9216,1024]{1,0:T(8,128)(2,1)}, s32[]{:T(128)}, bf16[2,64,1024]{2,1,0:T(8,128)(2,1)S(1)}, f32[2,2048]{1,0:T(2,128)}) %tuple.118), branch_computations={%region_16.16_spmd, %region_17.27_spmd} | conditional | flops 1212638592 | bytes 25697282 | solution.py:157
  345.3 13.2 %fusion.33 = bf16[1,8,8,9216]{3,2,1,0:T(8,128)(2,1)} fusion(bf16[64,1024]{1,0:T(8,128)(2,1)S(1)} %get-tuple-element.380, bf16[9216,1024]{1,0:T(8,128)(2,1)} %get-tuple-element.381), kind=kOutput, calls=%fused_computation.57 | convolution fusion | flops 1208549376 | bytes 20185088 | tf_op jit(solution)/shard_map/while/body/eval_jaxpr/cond/branch_1_fun/transpose(jvp())/dot_general | solution.py:98
  358.5 2.2 fusion.94
  362.4 3.0 multiply_reduce_fusion
  377.8 2.0 collective-permute-start.1
  381.4 1.5 collective-permute-done.1
  383.9 40.2 %conditional.5 = (bf16[64,1024]{1,0:T(8,128)(2,1)S(1)}) conditional(s32[]{:T(128)} %convert_element_type.246, bf16[64,1024]{1,0:T(8,128)(2,1)S(1)} %bitcast_select_fusion.7, (bf16[64,1024]{1,0:T(8,128)(2,1)S(1)}, bf16[9216,1024]{1,0:T(8,128)(2,1)}, s32[]{:T(128)}, bf16[2,64,1024]{2,1,0:T(8,128)(2,1)S(1)}, f32[2,2048]{1,0:T(2,128)}) %tuple.118), branch_computations={%region_16.16_spmd, %region_17.27_spmd} | conditional | flops 1212638592 | bytes 25697282 | solution.py:157
  391.5 13.2 %fusion.33 = bf16[1,8,8,9216]{3,2,1,0:T(8,128)(2,1)} fusion(bf16[64,1024]{1,0:T(8,128)(2,1)S(1)} %get-tuple-element.380, bf16[9216,1024]{1,0:T(8,128)(2,1)} %get-tuple-element.381), kind=kOutput, calls=%fused_computation.57 | convolution fusion | flops 1208549376 | bytes 20185088 | tf_op jit(solution)/shard_map/while/body/eval_jaxpr/cond/branch_1_fun/transpose(jvp())/dot_general | solution.py:98
  404.8 2.2 fusion.94
  408.7 3.0 multiply_reduce_fusion
  425.7 3.5 collective-permute-done.1
  429.2 1.7 broadcast_select_fusion
  431.6 3.3 copy.24
  434.9 3.4 copy.25
  438.3 3.4 copy.26
  441.6 3.4 copy.27
  445.0 24.0 %all-reduce.16.cloned.1.call-done = (bf16[2,64,1024]{2,1,0:T(8,128)(2,1)}, bf16[2,64,1024]{2,1,0:T(8,128)(2,1)}) async-done(((bf16[2,64,1024]{2,1,0:T(8,128)(2,1)}, bf16[2,64,1024]{2,1,0:T(8,128)(2,1)}), (bf16[2,64,1024]{2,1,0:T(8,128)(2,1)}, bf16[2,64,1024]{2,1,0:T(8,128)(2,1)})) %all-reduce.16.cloned.1.call-update) | async-done | bytes 524304 | tf_op jit(solution)/shard_map/psum | solution.py:41
  469.1 3.7 multiply_reduce_fusion.5
  472.8 4.9 %psum.39 = bf16[2,2]{0,1:T(2,128)(2,1)S(1)} all-reduce(bf16[2,2]{0,1:T(2,128)(2,1)S(1)} %pad_maximum_fusion.1), channel_id=1, replica_groups=mesh['section'=2,'batch'=16] {'section'}, use_global_device_ids=true, to_apply=%region_34.35 | all-reduce | flops 4 | bytes 16 | tf_op jit(solution)/shard_map/psum | solution.py:119
  478.4 2.7 fusion.79
  (211 shorter events, 91.2 us)
Async XLA Ops:
  7.2 118.5 %copy-start = (bf16[1024,1536]{1,0:T(8,128)(2,1)S(1)}, bf16[1024,1536]{1,0:T(8,128)(2,1)}, u32[]{:S(2)}) copy-start(bf16[1024,1536]{1,0:T(8,128)(2,1)} %param.28) | copy-start | bytes 9437188
  7.2 64.5 %copy-start.10 = (f32[3,3]{1,0:T(4,128)S(1)}, f32[3,3]{1,0:T(4,128)}, u32[]{:S(2)}) copy-start(f32[3,3]{1,0:T(4,128)} %constant.332) | copy-start | bytes 112
  7.2 64.4 %copy-start.13 = (f32[2]{0:T(128)S(1)}, f32[2]{0:T(128)}, u32[]{:S(2)}) copy-start(f32[2]{0:T(128)} %param.22) | copy-start | bytes 28
  7.2 64.4 %copy-start.11 = (f32[2]{0:T(128)S(1)}, f32[2]{0:T(128)}, u32[]{:S(2)}) copy-start(f32[2]{0:T(128)} %param.23) | copy-start | bytes 28
  7.2 209.0 %all-reduce.18.cloned.1.call-start = ((), (), s32[]{:S(2)}) async-start(), calls=%async_computation.1 | async-start | bytes 1048576 | tf_op jit(solution)/shard_map/psum | solution.py:119
  7.3 19.7 %collective-permute-start.2 = (bf16[1,576,1024]{2,1,0:T(8,128)(2,1)}, bf16[1,576,1024]{2,1,0:T(8,128)(2,1)S(1)}, u32[]{:S(2)}, u32[]{:S(2)}) collective-permute-start(bf16[1,576,1024]{2,1,0:T(8,128)(2,1)} %param.26), channel_id=1, source_target_pairs={{0,1},{1,2},{2,3},{3,4},{4,5},{5,6},{6,7},{7,8},{8,9},{9,10},{10,1... | collective-permute-start | bytes 3538952 | tf_op jit(solution)/shard_map/ppermute | solution.py:23
  7.8 29.7 %collective-permute-start.3 = (bf16[1,576,1024]{2,1,0:T(8,128)(2,1)}, bf16[1,576,1024]{2,1,0:T(8,128)(2,1)}, u32[]{:S(2)}, u32[]{:S(2)}) collective-permute-start(bf16[1,576,1024]{2,1,0:T(8,128)(2,1)} %param.26), channel_id=1, source_target_pairs={{0,15},{1,0},{2,1},{3,2},{4,3},{5,4},{6,5},{7,6},{8,7},{9,8},{10,9... | collective-permute-start | bytes 3538952 | tf_op jit(solution)/shard_map/ppermute | solution.py:26
  26.9 1.0 copy-start.4
  28.0 18.5 %collective-permute-start.4 = (bf16[1,576,1024]{2,1,0:T(8,128)(2,1)S(1)}, bf16[1,576,1024]{2,1,0:T(8,128)(2,1)}, u32[]{:S(2)}, u32[]{:S(2)}) collective-permute-start(bf16[1,576,1024]{2,1,0:T(8,128)(2,1)S(1)} %collective-permute-done.2), channel_id=1, source_target_pairs={{0,1},{1,2},{2,3},{3,4},{4,5},{5,6},{6,7},{7,8},{8,9},{9,10},{10,1... | collective-permute-start | bytes 3538952 | tf_op jit(solution)/shard_map/ppermute | solution.py:23
  37.5 34.2 %collective-permute-start.5 = (bf16[1,576,1024]{2,1,0:T(8,128)(2,1)}, bf16[1,576,1024]{2,1,0:T(8,128)(2,1)}, u32[]{:S(2)}, u32[]{:S(2)}) collective-permute-start(bf16[1,576,1024]{2,1,0:T(8,128)(2,1)} %collective-permute-done.3), channel_id=1, source_target_pairs={{0,15},{1,0},{2,1},{3,2},{4,3},{5,4},{6,5},{7,6},{8,7},{9,8},{10,9... | collective-permute-start | bytes 3538952 | tf_op jit(solution)/shard_map/ppermute | solution.py:26
  46.5 36.0 %collective-permute-start.6 = (bf16[1,576,1024]{2,1,0:T(8,128)(2,1)}, bf16[1,576,1024]{2,1,0:T(8,128)(2,1)}, u32[]{:S(2)}, u32[]{:S(2)}) collective-permute-start(bf16[1,576,1024]{2,1,0:T(8,128)(2,1)} %collective-permute-done.4), channel_id=1, source_target_pairs={{0,1},{1,2},{2,3},{3,4},{4,5},{5,6},{6,7},{7,8},{8,9},{9,10},{10,1... | collective-permute-start | bytes 3538952 | tf_op jit(solution)/shard_map/ppermute | solution.py:23
  71.7 23.2 %collective-permute-start.7 = (bf16[1,576,1024]{2,1,0:T(8,128)(2,1)}, bf16[1,576,1024]{2,1,0:T(8,128)(2,1)}, u32[]{:S(2)}, u32[]{:S(2)}) collective-permute-start(bf16[1,576,1024]{2,1,0:T(8,128)(2,1)} %collective-permute-done.5), channel_id=1, source_target_pairs={{0,15},{1,0},{2,1},{3,2},{4,3},{5,4},{6,5},{7,6},{8,7},{9,8},{10,9... | collective-permute-start | bytes 3538952 | tf_op jit(solution)/shard_map/ppermute | solution.py:26
  75.3 19.8 %copy-start.1 = (bf16[2,64,1536]{2,1,0:T(8,128)(2,1)S(1)}, bf16[2,64,1536]{2,1,0:T(8,128)(2,1)}, u32[]{:S(2)}) copy-start(bf16[2,64,1536]{2,1,0:T(8,128)(2,1)} %param.21) | copy-start | bytes 1179652
  82.5 22.5 %collective-permute-start.8 = (bf16[1,576,1024]{2,1,0:T(8,128)(2,1)}, bf16[1,576,1024]{2,1,0:T(8,128)(2,1)}, u32[]{:S(2)}, u32[]{:S(2)}) collective-permute-start(bf16[1,576,1024]{2,1,0:T(8,128)(2,1)} %collective-permute-done.6), channel_id=1, source_target_pairs={{0,1},{1,2},{2,3},{3,4},{4,5},{5,6},{6,7},{7,8},{8,9},{9,10},{10,1... | collective-permute-start | bytes 3538952 | tf_op jit(solution)/shard_map/ppermute | solution.py:23
  94.9 30.7 %copy-start.6 = (f32[2]{0:T(128)}, f32[2]{0:T(128)S(1)}, u32[]{:S(2)}) copy-start(f32[2]{0:T(128)S(1)} %get-tuple-element.477) | copy-start | bytes 28
  95.0 30.7 %copy-start.8 = (f32[2]{0:T(128)}, f32[2]{0:T(128)S(1)}, u32[]{:S(2)}) copy-start(f32[2]{0:T(128)S(1)} %get-tuple-element.479) | copy-start | bytes 28
  95.0 32.8 %collective-permute-start.9 = (bf16[1,576,1024]{2,1,0:T(8,128)(2,1)}, bf16[1,576,1024]{2,1,0:T(8,128)(2,1)}, u32[]{:S(2)}, u32[]{:S(2)}) collective-permute-start(bf16[1,576,1024]{2,1,0:T(8,128)(2,1)} %collective-permute-done.7), channel_id=1, source_target_pairs={{0,15},{1,0},{2,1},{3,2},{4,3},{5,4},{6,5},{7,6},{8,7},{9,8},{10,9... | collective-permute-start | bytes 3538952 | tf_op jit(solution)/shard_map/ppermute | solution.py:26
  105.0 26.3 %collective-permute-start.10 = (bf16[1,576,1024]{2,1,0:T(8,128)(2,1)}, bf16[1,576,1024]{2,1,0:T(8,128)(2,1)}, u32[]{:S(2)}, u32[]{:S(2)}) collective-permute-start(bf16[1,576,1024]{2,1,0:T(8,128)(2,1)} %collective-permute-done.8), channel_id=1, source_target_pairs={{0,1},{1,2},{2,3},{3,4},{4,5},{5,6},{6,7},{7,8},{8,9},{9,10},{10,1... | collective-permute-start | bytes 3538952 | tf_op jit(solution)/shard_map/ppermute | solution.py:23
  125.7 1.9 copy-start.12
  127.5 341.5 %all-reduce.16.cloned.1.call-start = ((), (), s32[]{:S(2)}) async-start(), calls=%async_computation | async-start | bytes 1048576 | tf_op jit(solution)/shard_map/psum | solution.py:41
  127.8 38.3 %collective-permute-start.11 = (bf16[1,576,1024]{2,1,0:T(8,128)(2,1)}, bf16[1,576,1024]{2,1,0:T(8,128)(2,1)}, u32[]{:S(2)}, u32[]{:S(2)}) collective-permute-start(bf16[1,576,1024]{2,1,0:T(8,128)(2,1)} %collective-permute-done.9), channel_id=1, source_target_pairs={{0,15},{1,0},{2,1},{3,2},{4,3},{5,4},{6,5},{7,6},{8,7},{9,8},{10,9... | collective-permute-start | bytes 3538952 | tf_op jit(solution)/shard_map/ppermute | solution.py:26
  131.3 26.5 %copy-start.3 = (bf16[1,576,1024]{2,1,0:T(8,128)(2,1)S(1)}, bf16[1,576,1024]{2,1,0:T(8,128)(2,1)}, u32[]{:S(2)}) copy-start(bf16[1,576,1024]{2,1,0:T(8,128)(2,1)} %param.26) | copy-start | bytes 3538948
  131.3 37.2 %collective-permute-start.12 = (bf16[1,576,1024]{2,1,0:T(8,128)(2,1)}, bf16[1,576,1024]{2,1,0:T(8,128)(2,1)}, u32[]{:S(2)}, u32[]{:S(2)}) collective-permute-start(bf16[1,576,1024]{2,1,0:T(8,128)(2,1)} %collective-permute-done.10), channel_id=1, source_target_pairs={{0,1},{1,2},{2,3},{3,4},{4,5},{5,6},{6,7},{7,8},{8,9},{9,10},{10,1... | collective-permute-start | bytes 3538952 | tf_op jit(solution)/shard_map/ppermute | solution.py:23
  166.1 14.4 %collective-permute-start.13 = (bf16[1,576,1024]{2,1,0:T(8,128)(2,1)}, bf16[1,576,1024]{2,1,0:T(8,128)(2,1)S(1)}, u32[]{:S(2)}, u32[]{:S(2)}) collective-permute-start(bf16[1,576,1024]{2,1,0:T(8,128)(2,1)} %collective-permute-done.11), channel_id=1, source_target_pairs={{0,15},{1,0},{2,1},{3,2},{4,3},{5,4},{6,5},{7,6},{8,7},{9,8},{10,9... | collective-permute-start | bytes 3538952 | tf_op jit(solution)/shard_map/ppermute | solution.py:26
  168.5 18.7 %collective-permute-start.14 = (bf16[1,576,1024]{2,1,0:T(8,128)(2,1)}, bf16[1,576,1024]{2,1,0:T(8,128)(2,1)S(1)}, u32[]{:S(2)}, u32[]{:S(2)}) collective-permute-start(bf16[1,576,1024]{2,1,0:T(8,128)(2,1)} %collective-permute-done.12), channel_id=1, source_target_pairs={{0,1},{1,2},{2,3},{3,4},{4,5},{5,6},{6,7},{7,8},{8,9},{9,10},{10,1... | collective-permute-start | bytes 3538952 | tf_op jit(solution)/shard_map/ppermute | solution.py:23
  180.5 33.0 %collective-permute-start.15 = (bf16[1,576,1024]{2,1,0:T(8,128)(2,1)S(1)}, bf16[1,576,1024]{2,1,0:T(8,128)(2,1)S(1)}, u32[]{:S(2)}, u32[]{:S(2)}) collective-permute-start(bf16[1,576,1024]{2,1,0:T(8,128)(2,1)S(1)} %collective-permute-done.13), channel_id=1, source_target_pairs={{0,15},{1,0},{2,1},{3,2},{4,3},{5,4},{6,5},{7,6},{8,7},{9,8},{10,9... | collective-permute-start | bytes 3538952 | tf_op jit(solution)/shard_map/ppermute | solution.py:26
  187.2 27.9 %collective-permute-start.16 = (bf16[1,576,1024]{2,1,0:T(8,128)(2,1)S(1)}, bf16[1,576,1024]{2,1,0:T(8,128)(2,1)S(1)}, u32[]{:S(2)}, u32[]{:S(2)}) collective-permute-start(bf16[1,576,1024]{2,1,0:T(8,128)(2,1)S(1)} %collective-permute-done.14), channel_id=1, source_target_pairs={{0,1},{1,2},{2,3},{3,4},{4,5},{5,6},{6,7},{7,8},{8,9},{9,10},{10,1... | collective-permute-start | bytes 3538952 | tf_op jit(solution)/shard_map/ppermute | solution.py:23
  236.9 5.1 %collective-permute-start = (bf16[64,1024]{1,0:T(8,128)(2,1)S(1)}, bf16[64,1024]{1,0:T(8,128)(2,1)}, u32[]{:S(2)}, u32[]{:S(2)}) collective-permute-start(bf16[64,1024]{1,0:T(8,128)(2,1)S(1)} %get-tuple-element.674), channel_id=1, source_target_pairs={{0,16},{16,0},{1,17},{17,1},{2,18},{18,2},{3,19},{19,3},{4,20},{20... | collective-permute-start | bytes 393224 | tf_op jit(solution)/shard_map/while/body/eval_jaxpr/ppermute | solution.py:36
  261.3 5.1 %collective-permute-start = (bf16[64,1024]{1,0:T(8,128)(2,1)S(1)}, bf16[64,1024]{1,0:T(8,128)(2,1)}, u32[]{:S(2)}, u32[]{:S(2)}) collective-permute-start(bf16[64,1024]{1,0:T(8,128)(2,1)S(1)} %get-tuple-element.674), channel_id=1, source_target_pairs={{0,16},{16,0},{1,17},{17,1},{2,18},{18,2},{3,19},{19,3},{4,20},{20... | collective-permute-start | bytes 393224 | tf_op jit(solution)/shard_map/while/body/eval_jaxpr/ppermute | solution.py:36
  267.5 21.5 %collective-permute-start = (bf16[64,1024]{1,0:T(8,128)(2,1)S(1)}, bf16[64,1024]{1,0:T(8,128)(2,1)}, u32[]{:S(2)}, u32[]{:S(2)}) collective-permute-start(bf16[64,1024]{1,0:T(8,128)(2,1)S(1)} %get-tuple-element.674), channel_id=1, source_target_pairs={{0,16},{16,0},{1,17},{17,1},{2,18},{18,2},{3,19},{19,3},{4,20},{20... | collective-permute-start | bytes 393224 | tf_op jit(solution)/shard_map/while/body/eval_jaxpr/ppermute | solution.py:36
  291.4 45.2 %collective-permute-start.1 = (bf16[64,1024]{1,0:T(8,128)(2,1)S(1)}, bf16[64,1024]{1,0:T(8,128)(2,1)}, u32[]{:S(2)}, u32[]{:S(2)}) collective-permute-start(bf16[64,1024]{1,0:T(8,128)(2,1)S(1)} %get-tuple-element.675), channel_id=1, source_target_pairs={{0,16},{16,0},{1,17},{17,1},{2,18},{18,2},{3,19},{19,3},{4,20},{20... | collective-permute-start | bytes 393224 | tf_op jit(solution)/shard_map/while/body/eval_jaxpr/ppermute | solution.py:36
  343.3 0.5 copy-start.5
  377.8 5.1 %collective-permute-start.1 = (bf16[64,1024]{1,0:T(8,128)(2,1)S(1)}, bf16[64,1024]{1,0:T(8,128)(2,1)}, u32[]{:S(2)}, u32[]{:S(2)}) collective-permute-start(bf16[64,1024]{1,0:T(8,128)(2,1)S(1)} %get-tuple-element.675), channel_id=1, source_target_pairs={{0,16},{16,0},{1,17},{17,1},{2,18},{18,2},{3,19},{19,3},{4,20},{20... | collective-permute-start | bytes 393224 | tf_op jit(solution)/shard_map/while/body/eval_jaxpr/ppermute | solution.py:36
  389.6 0.5 copy-start.5
  424.0 5.1 %collective-permute-start.1 = (bf16[64,1024]{1,0:T(8,128)(2,1)S(1)}, bf16[64,1024]{1,0:T(8,128)(2,1)}, u32[]{:S(2)}, u32[]{:S(2)}) collective-permute-start(bf16[64,1024]{1,0:T(8,128)(2,1)S(1)} %get-tuple-element.675), channel_id=1, source_target_pairs={{0,16},{16,0},{1,17},{17,1},{2,18},{18,2},{3,19},{19,3},{4,20},{20... | collective-permute-start | bytes 393224 | tf_op jit(solution)/shard_map/while/body/eval_jaxpr/ppermute | solution.py:36
  438.3 30.8 %copy-start.2 = (bf16[2,64,1536]{2,1,0:T(8,128)(2,1)S(1)}, bf16[2,64,1536]{2,1,0:T(8,128)(2,1)}, u32[]{:S(2)}) copy-start(bf16[2,64,1536]{2,1,0:T(8,128)(2,1)} %param.21) | copy-start | bytes 1179652
  438.3 30.8 %copy-start.7 = (f32[2]{0:T(128)S(1)}, f32[2]{0:T(128)}, u32[]{:S(2)}) copy-start(f32[2]{0:T(128)} %copy-done.6) | copy-start | bytes 28
  469.1 9.3 %copy-start.9 = (f32[2]{0:T(128)S(1)}, f32[2]{0:T(128)}, u32[]{:S(2)}) copy-start(f32[2]{0:T(128)} %copy-done.8) | copy-start | bytes 28
Sparse Core Ops, SparseCore 0:
  127.7 29.8 all-reduce.17
  431.7 37.2 all-reduce.15
